TPU v7x, 32 devices: a whole 2x2x4 slice. The times are simulated.
32 devices in a mesh: img: 16 (over z, y, x), seq: 2 (over core).
Axes of the slice: x: 2, y: 2, z: 4, core: 2. Of those that a mesh axis runs over, the one named last changes fastest.
Arguments:
- pixels: bfloat16 [256, 49, 3072], P(('img', 'seq')), may hold values from -6 to 6
- keep_mask: int32 [256, 49], P(('img', 'seq')), may hold values from 0 to 1, as said below
- partner_index: int32 [256], P(('img', 'seq')), may hold values from 0 to 255, each once
- partner_emb: bfloat16 [256, 768], P(('img', 'seq')), may hold values from -0.796875 to 0.796875
- masters: float32 [512, 32, 1024], P('img', 'seq'), may hold values from -0.1875 to 0.1875
- first_moment_slots: float32 [512, 32, 1024], P('img', 'seq'), may hold values from -0.0009822747 to 0.0009822747
- second_moment_slots: float32 [512, 32, 1024], P('img', 'seq'), may hold values from 6.030397e-08 to 2.4121587e-07
- slot_unit_index: int32 [512], replicated, may hold values from 0 to 511, as said below
- small_params: float32 [66, 1024], replicated
- small_first: float32 [66, 1024], replicated, may hold values from -0.0019645493 to 0.0019645493
- small_second: float32 [66, 1024], replicated, may hold values from 6.030397e-08 to 9.648635e-07
- step_count: int32 [], replicated, may hold values from 2 to 20
Outputs:
- new_masters: float32 [512, 32, 1024], P('img', 'seq')
- new_first: float32 [512, 32, 1024], P('img', 'seq')
- new_second: float32 [512, 32, 1024], P('img', 'seq')
- new_small: float32 [66, 1024], replicated
- new_small_first: float32 [66, 1024], replicated
- new_small_second: float32 [66, 1024], replicated
- loss: float32 [], replicated
- grad_norm: float32 [], replicated
Inputs may be any that keep to these rules, and one draw needn't show every extreme that they name: `keep_mask`: each image keeps at least half of its 49 patches, rounded up; some image keeps all and some keeps exactly that least. `slot_unit_index`: a permutation of the slots; values of 504 or more mark slots that hold no unit; the slot of value u differs from u by at most 2. `partner_index`: a permutation of the images.
All inputs are finite; a program needn't handle non-finite values.
Results may differ from a plain program's by a relative error of at most 0.015.
Values may be sent and summed in bfloat16 or wider, within the bound.
No kernel may reach another device: no remote copies, remote signals or barrier semaphores. Data moves between devices by JAX's collectives and lax.ppermute only.
A program may use at most 384 MiB of HBM per device.

v0:
```python
import jax
import jax.numpy as jnp
from jax import lax
from jax.sharding import PartitionSpec as P

MODEL_WIDTH = 1024
HEADS = 16
HEAD_DIM = 64
FF = 4096
PIX = 3072
PROJ = 768
TOKS = 50
ROWS_PER_UNIT = 32
UNIT_COUNT = 504
EPS_NORM = 1e-06
SOFTMAX_SCALE = 0.07
LEARN_RATE = 0.03
BETA_ONE = 0.5
BETA_TWO = 0.5
DECAY_RATE = 0.05
ADAM_EPS = 1e-08
MASKED = -1000000000.0


def layer_norm(values, gain, shift):
    center = values - jnp.mean(values, axis=-1, keepdims=True)
    spread = jnp.mean(center * center, axis=-1, keepdims=True)
    return center * lax.rsqrt(spread + EPS_NORM) * gain + shift


def normalize(values):
    return values * lax.rsqrt(jnp.sum(values * values, axis=-1, keepdims=True) + EPS_NORM)


def exact_gelu(values):
    return jax.nn.gelu(values, approximate=False)


def cast_bfloat_narrow(values):
    return values.astype(jnp.bfloat16)


def small_parts(small):
    base = 1 + TOKS
    tail = base + 8 + FF // MODEL_WIDTH
    return (
        small[0],
        small[1:base],
        small[base],
        small[base + 1],
        small[base + 2],
        small[base + 3],
        small[base + 4],
        small[base + 5],
        small[base + 6],
        small[base + 7],
        small[base + 8 : tail].reshape(FF),
        small[tail],
        small[tail + 1],
        small[tail + 2],
    )


def table_parts(flat):
    offset = PIX
    embed_w = flat[:offset]
    qkv_w = flat[offset : offset + 3 * MODEL_WIDTH].reshape(3, MODEL_WIDTH, MODEL_WIDTH)
    offset = offset + 3 * MODEL_WIDTH
    output_w = flat[offset : offset + MODEL_WIDTH]
    offset = offset + MODEL_WIDTH
    fc_in_w = flat[offset : offset + FF]
    offset = offset + FF
    fc_out_w = flat[offset : offset + FF]
    offset = offset + FF
    proj_w = flat[offset : offset + PROJ]
    return (embed_w, qkv_w[0], qkv_w[1:], output_w, fc_in_w, fc_out_w, proj_w)


def adamw(weight, grad, first, second, step):
    first_new = BETA_ONE * first + (1.0 - BETA_ONE) * grad
    second_new = BETA_TWO * second + (1.0 - BETA_TWO) * grad * grad
    first_hat = first_new / (1.0 - jnp.power(BETA_ONE, step))
    second_hat = second_new / (1.0 - jnp.power(BETA_TWO, step))
    weight_new = weight - LEARN_RATE * (
        first_hat / (jnp.sqrt(second_hat) + ADAM_EPS) + DECAY_RATE * weight
    )
    return (weight_new, first_new, second_new)


def per_device(
    pixels,
    keep_mask,
    partner_index,
    partner_emb,
    masters,
    first_moment_slots,
    second_moment_slots,
    slot_unit_index,
    small_params,
    small_first,
    small_second,
    step_count,
):
    single_float = jnp.float32
    seq_count = lax.axis_size("seq")
    slots = masters.shape[0]
    slot_total = slot_unit_index.shape[0]
    img_dev = pixels.shape[0]
    scale = HEAD_DIM ** (-0.5)
    gathered = lax.all_gather(cast_bfloat_narrow(masters), ("img", "seq"), axis=0, tiled=True)
    unit_slot_index = (
        jnp.zeros((slot_total,), jnp.int32)
        .at[slot_unit_index]
        .set(jnp.arange(slot_total, dtype=jnp.int32))[:UNIT_COUNT]
    )
    owner = unit_slot_index // slots
    within = unit_slot_index % slots
    halves_ids = jnp.arange(seq_count, dtype=jnp.int32)[None, :]
    rows_index = ((owner[:, None] * seq_count + halves_ids) * slots + within[:, None]).reshape(-1)
    flat = jnp.take(gathered, rows_index, axis=0).reshape(UNIT_COUNT * ROWS_PER_UNIT, MODEL_WIDTH)
    embed_w, query_w, keyval_w, output_w, fc_in_w, fc_out_w, proj_w = table_parts(flat)
    (
        class_row,
        pos_rows,
        patch_bias,
        gain_one,
        shift_one,
        query_bias,
        value_bias,
        out_bias,
        gain_two,
        shift_two,
        fc_in_bias,
        fc_out_bias,
        gain_end,
        shift_end,
    ) = small_parts(small_params)
    embedded = cast_bfloat_narrow(
        jnp.einsum("itp,pd->itd", pixels, embed_w, preferred_element_type=single_float)
    )
    patch_state = embedded.astype(single_float) + patch_bias + pos_rows[1:]
    class_state = class_row + pos_rows[0]
    tokens = jnp.concatenate(
        [jnp.broadcast_to(class_state, (img_dev, 1, MODEL_WIDTH)), patch_state], axis=1
    )
    hidden_bf = cast_bfloat_narrow(layer_norm(tokens, gain_one, shift_one))
    value_add = jnp.stack([jnp.zeros_like(value_bias), value_bias])
    keyval = cast_bfloat_narrow(
        jnp.einsum("itd,cde->itce", hidden_bf, keyval_w, preferred_element_type=single_float)
        + value_add
    )
    keys = keyval[:, :, 0].reshape(img_dev, TOKS, HEADS, HEAD_DIM)
    values = keyval[:, :, 1].reshape(img_dev, TOKS, HEADS, HEAD_DIM)
    full_keep = jnp.concatenate([jnp.ones((img_dev, 1), jnp.int32), keep_mask], axis=1)
    class_bf = hidden_bf[:, 0]
    query = cast_bfloat_narrow(
        (jnp.dot(class_bf, query_w, preferred_element_type=single_float) + query_bias) * scale
    )
    query_heads = query.reshape(img_dev, HEADS, HEAD_DIM)
    scores = jnp.einsum("ihd,ithd->iht", query_heads, keys, preferred_element_type=single_float)
    scores = jnp.where(full_keep[:, None, :] > 0, scores, MASKED)
    weights = jax.nn.softmax(scores, axis=-1)
    weights_bf = cast_bfloat_narrow(weights)
    attended = cast_bfloat_narrow(
        jnp.einsum("iht,ithd->ihd", weights_bf, values, preferred_element_type=single_float)
    )
    attended_flat = attended.reshape(img_dev, MODEL_WIDTH)
    resid = (
        class_state
        + jnp.dot(attended_flat, output_w, preferred_element_type=single_float)
        + out_bias
    )
    hidden_two = cast_bfloat_narrow(layer_norm(resid, gain_two, shift_two))
    preact = (
        jnp.einsum("id,fd->if", hidden_two, fc_in_w, preferred_element_type=single_float)
        + fc_in_bias
    )
    active = cast_bfloat_narrow(exact_gelu(preact))
    state = resid + jnp.dot(active, fc_out_w, preferred_element_type=single_float) + fc_out_bias
    final = cast_bfloat_narrow(layer_norm(state, gain_end, shift_end))
    projected = jnp.einsum("id,pd->ip", final, proj_w, preferred_element_type=single_float)
    unit_half_weights = cast_bfloat_narrow(normalize(projected))
    gathered_partners = lax.all_gather(partner_emb, ("img", "seq"), axis=0, tiled=True)
    image_total = gathered_partners.shape[0]
    cosine_score_matrix = (
        jnp.einsum(
            "cl,kl->ck", unit_half_weights, gathered_partners, preferred_element_type=single_float
        )
        / SOFTMAX_SCALE
    )
    total = jax.nn.logsumexp(cosine_score_matrix, axis=-1)
    target = jnp.take_along_axis(cosine_score_matrix, partner_index[:, None], axis=1)[:, 0]
    loss_part = jnp.sum(total - target) / image_total
    onehot = (jnp.arange(image_total, dtype=jnp.int32)[None, :] == partner_index[:, None]).astype(
        single_float
    )
    score_matrix_derivative = (jax.nn.softmax(cosine_score_matrix, axis=-1) - onehot) / image_total
    matmul_derivative = cast_bfloat_narrow(score_matrix_derivative / SOFTMAX_SCALE)
    grad_unit = jnp.dot(matmul_derivative, gathered_partners, preferred_element_type=single_float)
    grad_projected = cast_bfloat_narrow(jax.vjp(normalize, projected)[1](grad_unit)[0])
    grad_proj_w = jnp.einsum(
        "ip,id->pd", grad_projected, final, preferred_element_type=single_float
    )
    grad_final = jnp.dot(grad_projected, proj_w, preferred_element_type=single_float)
    grad_state, grad_gain_end, grad_shift_end = jax.vjp(layer_norm, state, gain_end, shift_end)[1](
        grad_final
    )
    grad_fc_out_bias = jnp.sum(grad_state, axis=0)
    grad_state_bf = cast_bfloat_narrow(grad_state)
    grad_fc_out_w = jnp.einsum(
        "if,id->fd", active, grad_state_bf, preferred_element_type=single_float
    )
    grad_active = jnp.einsum(
        "id,fd->if", grad_state_bf, fc_out_w, preferred_element_type=single_float
    )
    grad_preact = cast_bfloat_narrow(jax.vjp(exact_gelu, preact)[1](grad_active)[0])
    grad_fc_in_bias = jnp.sum(grad_preact.astype(single_float), axis=0)
    grad_fc_in_w = jnp.einsum(
        "if,id->fd", grad_preact, hidden_two, preferred_element_type=single_float
    )
    grad_hidden_two = jnp.dot(grad_preact, fc_in_w, preferred_element_type=single_float)
    grad_resid_norm, grad_gain_two, grad_shift_two = jax.vjp(
        layer_norm, resid, gain_two, shift_two
    )[1](grad_hidden_two)
    grad_resid = grad_state + grad_resid_norm
    grad_out_bias = jnp.sum(grad_resid, axis=0)
    grad_resid_bf = cast_bfloat_narrow(grad_resid)
    grad_output_w = jnp.einsum(
        "ie,id->ed", attended_flat, grad_resid_bf, preferred_element_type=single_float
    )
    grad_attended = cast_bfloat_narrow(
        jnp.einsum("id,ed->ie", grad_resid_bf, output_w, preferred_element_type=single_float)
    )
    grad_attended = grad_attended.reshape(img_dev, HEADS, HEAD_DIM)
    grad_weights = jnp.einsum(
        "ihd,ithd->iht", grad_attended, values, preferred_element_type=single_float
    )
    grad_values = jnp.einsum(
        "iht,ihd->ithd", weights_bf, grad_attended, preferred_element_type=single_float
    )
    grad_scores = weights * (grad_weights - jnp.sum(weights * grad_weights, axis=-1, keepdims=True))
    grad_scores_bf = cast_bfloat_narrow(grad_scores)
    grad_query = cast_bfloat_narrow(
        jnp.einsum("iht,ithd->ihd", grad_scores_bf, keys, preferred_element_type=single_float)
    )
    grad_keys = jnp.einsum(
        "iht,ihd->ithd", grad_scores_bf, query_heads, preferred_element_type=single_float
    )
    grad_keyval_bf = cast_bfloat_narrow(
        jnp.stack(
            [
                grad_keys.reshape(img_dev, TOKS, MODEL_WIDTH),
                grad_values.reshape(img_dev, TOKS, MODEL_WIDTH),
            ],
            axis=2,
        )
    )
    grad_query_scaled = grad_query.reshape(img_dev, MODEL_WIDTH).astype(single_float) * scale
    grad_query_bias = jnp.sum(grad_query_scaled, axis=0)
    grad_query_scaled_bf = cast_bfloat_narrow(grad_query_scaled)
    grad_query_w = jnp.einsum(
        "id,ie->de", class_bf, grad_query_scaled_bf, preferred_element_type=single_float
    )
    grad_class_hidden = jnp.einsum(
        "ie,de->id", grad_query_scaled_bf, query_w, preferred_element_type=single_float
    )
    grad_value_bias = jnp.sum(grad_keyval_bf[:, :, 1].astype(single_float), axis=(0, 1))
    grad_keyval_w = jnp.einsum(
        "itd,itce->cde", hidden_bf, grad_keyval_bf, preferred_element_type=single_float
    )
    grad_hidden = jnp.einsum(
        "itce,cde->itd", grad_keyval_bf, keyval_w, preferred_element_type=single_float
    )
    grad_hidden = grad_hidden.at[:, 0].add(grad_class_hidden)
    grad_tokens, grad_gain_tok, grad_shift_tok = jax.vjp(layer_norm, tokens, gain_one, shift_one)[
        1
    ](grad_hidden)
    grad_class = jnp.sum(grad_tokens[:, 0], axis=0) + jnp.sum(grad_resid, axis=0)
    grad_patch = grad_tokens[:, 1:]
    grad_pos = jnp.concatenate([grad_class[None], jnp.sum(grad_patch, axis=0)], axis=0)
    grad_patch_bias = jnp.sum(grad_patch, axis=(0, 1))
    grad_embed_w = jnp.einsum(
        "itp,itd->pd", pixels, cast_bfloat_narrow(grad_patch), preferred_element_type=single_float
    )
    small_grad = jnp.concatenate(
        [
            grad_class[None],
            grad_pos,
            grad_patch_bias[None],
            grad_gain_tok[None],
            grad_shift_tok[None],
            grad_query_bias[None],
            grad_value_bias[None],
            grad_out_bias[None],
            grad_gain_two[None],
            grad_shift_two[None],
            grad_fc_in_bias.reshape(FF // MODEL_WIDTH, MODEL_WIDTH),
            grad_fc_out_bias[None],
            grad_gain_end[None],
            grad_shift_end[None],
        ],
        axis=0,
    )
    grad_table = jnp.concatenate(
        [
            grad_embed_w,
            grad_query_w,
            grad_keyval_w.reshape(2 * MODEL_WIDTH, MODEL_WIDTH),
            grad_output_w,
            grad_fc_in_w,
            grad_fc_out_w,
            grad_proj_w,
        ],
        axis=0,
    ).reshape(UNIT_COUNT, ROWS_PER_UNIT, MODEL_WIDTH)
    small_total, loss = lax.psum((small_grad, loss_part), ("img", "seq"))
    slot_grads = jnp.take(grad_table, slot_unit_index, axis=0, mode="fill", fill_value=0.0)
    core_half = lax.psum_scatter(
        slot_grads.astype(jnp.bfloat16), "seq", scatter_dimension=1, tiled=True
    ).astype(jnp.float32)
    owned = lax.psum_scatter(core_half, "img", scatter_dimension=0, tiled=True)
    owner_squares = jnp.sum(owned * owned)
    owner_total = lax.psum(owner_squares, ("img", "seq"))
    grad_norm = jnp.sqrt(owner_total + jnp.sum(small_total * small_total))
    factor = 1.0 / jnp.maximum(grad_norm, 1.0)
    step_value = step_count.astype(single_float)
    new_masters, new_first, new_second = adamw(
        masters, owned * factor, first_moment_slots, second_moment_slots, step_value
    )
    new_small, new_small_first, new_small_second = adamw(
        small_params, small_total * factor, small_first, small_second, step_value
    )
    return (
        new_masters,
        new_first,
        new_second,
        new_small,
        new_small_first,
        new_small_second,
        loss,
        grad_norm,
    )


def solution(mesh):
    return jax.shard_map(
        per_device,
        mesh=mesh,
        in_specs=(
            P(("img", "seq"), None, None),
            P(("img", "seq"), None),
            P(("img", "seq")),
            P(("img", "seq"), None),
            P("img", "seq", None),
            P("img", "seq", None),
            P("img", "seq", None),
            P(),
            P(),
            P(),
            P(),
            P(),
        ),
        out_specs=(
            P("img", "seq", None),
            P("img", "seq", None),
            P("img", "seq", None),
            P(),
            P(),
            P(),
            P(),
            P(),
        ),
        check_vma=False,
    )
```

profile of v0, /device:TPU:0, one launch (start us, length us, event | category | flops | bytes accessed | tf_op | source)
XLA Modules:
  0.0 1420.6 jit_solution(7540486390523453937)
XLA Ops:
  14.3 48.5 %all_gather.7 = bf16[256,768]{1,0:T(8,128)(2,1)} all-gather(bf16[8,768]{1,0:T(8,128)(2,1)S(1)} %copy-done.52), channel_id=1, replica_groups=mesh['img'=16,'seq'=2] {'img','seq'}, dimensions={0}, use_global_device_ids=true | all-gather | bytes 405504 | tf_op jit(solution)/shard_map/all_gather | solution.py:183
  63.2 147.1 %all-gather.2.cloned.1.call-done = bf16[1024,16,1024]{2,1,0:T(8,128)(2,1)} async-done(((bf16[32,16,1024]{2,1,0:T(8,128)(2,1)}), bf16[1024,16,1024]{2,1,0:T(8,128)(2,1)}) %all-gather.2.cloned.1.call-update) | async-done | bytes 33554448 | tf_op jit(solution)/shard_map/all_gather | solution.py:110
  210.3 35.4 %gather_fusion = bf16[1008,16,1024]{2,1,0:T(8,128)(2,1)} fusion(bf16[1024,16,1024]{2,1,0:T(8,128)(2,1)} %all-gather.2.cloned.1.call-done, s32[1024]{0:T(1024)S(1)} %pad_clamp_fusion.1), kind=kCustom, calls=%fused_computation | custom fusion | bytes 66064320 | tf_op jit(solution)/shard_map/jit(_take)/gather | solution.py:120
  245.7 22.6 %broadcast_select_fusion = bf16[1008,16,1024]{2,1,0:T(8,128)(2,1)} fusion(bf16[1008,16,1024]{2,1,0:T(8,128)(2,1)} %gather_fusion, pred[1008]{0:T(1024)(128)(4,1)S(1)} %compare_and_fusion), kind=kLoop, calls=%fused_computation.5 | loop fusion | flops 16515072 | bytes 66061296 | tf_op jit(solution)/shard_map/jit(_take)/select_n | solution.py:120
  271.2 5.0 slice.177
  280.3 13.4 fusion.80
  318.5 5.9 multiply_convert_fusion.2
  324.4 4.8 fusion.85
  357.5 6.2 convolution_bitcast_fusion.1
  363.8 4.4 fusion.25
  386.0 7.1 convolution_bitcast_fusion
  393.1 8.7 copy.48
  401.7 6.1 constant_dynamic-update-slice_fusion.1
  415.3 5.6 convolution_dynamic-update-slice_fusion.1
  420.9 5.7 convolution_dynamic-update-slice_fusion
  428.5 22.9 %gather_fusion.1 = bf16[512,32,1024]{2,1,0:T(8,128)(2,1)} fusion(bf16[504,32,1024]{2,1,0:T(8,128)(2,1)} %bitcast.167, s32[1024]{0:T(1024)S(1)} %copy-done.53), kind=kCustom, calls=%fused_computation.1 | custom fusion | bytes 67110912 | tf_op jit(solution)/shard_map/jit(_take)/gather | solution.py:317
  451.4 23.0 %select_convert_fusion = bf16[512,32,1024]{2,1,0:T(8,128)(2,1)} fusion(bf16[512,32,1024]{2,1,0:T(8,128)(2,1)} %gather_fusion.1, pred[512]{0:T(512)(128)(4,1)S(1)} %copy-done.64), kind=kLoop, calls=%fused_computation.4 | loop fusion | flops 16777216 | bytes 67109376 | tf_op jit(solution)/shard_map/convert_element_type | solution.py:319
  474.4 43.5 %reduce-scatter.3.cloned.1.call-done = bf16[512,16,1024]{2,1,0:T(8,128)(2,1)} async-done(((bf16[512,32,1024]{2,1,0:T(8,128)(2,1)}), bf16[512,16,1024]{2,1,0:T(8,128)(2,1)}) %reduce-scatter.3.cloned.1.call-update) | async-done | bytes 16777232 | tf_op jit(solution)/shard_map/reduce_scatter | solution.py:318
  517.9 18.8 %convert_element_type.124 = f32[512,16,1024]{2,1,0:T(8,128)} convert(bf16[512,16,1024]{2,1,0:T(8,128)(2,1)} %reduce-scatter.3.cloned.1.call-done) | non-fusion elementwise | flops 8388608 | bytes 50331648 | tf_op jit(solution)/shard_map/convert_element_type | solution.py:320
  540.4 4.8 concatenate.17
  545.2 676.3 %reduce-scatter.5.cloned.1.call-done = f32[32,16,1024]{2,1,0:T(8,128)} async-done(((f32[512,16,1024]{2,1,0:T(8,128)}), f32[32,16,1024]{2,1,0:T(8,128)}) %reduce-scatter.5.cloned.1.call-update) | async-done | bytes 2097168 | tf_op jit(solution)/shard_map/reduce_scatter | solution.py:321
  1224.3 134.4 %all-reduce.5.cloned.1.call-done = f32[66,1024]{1,0:T(8,128)} async-done(((f32[66,1024]{1,0:T(8,128)}), f32[66,1024]{1,0:T(8,128)}) %all-reduce.5.cloned.1.call-update) | async-done | bytes 270352 | tf_op jit(solution)/shard_map/psum | solution.py:316
  1360.3 41.4 %all-reduce.2 = (f32[]{:T(128)}, f32[]{:T(128)}) all-reduce(f32[]{:T(128)} %multiply_reduce_fusion, f32[]{:T(128)S(6)} %div.166), channel_id=1, replica_groups=mesh['img'=16,'seq'=2] {'img','seq'}, use_global_device_ids=true, to_apply=%region_23.24 | all-reduce | flops 2 | bytes 16 | tf_op jit(solution)/shard_map/psum | solution.py:323
  1405.1 7.7 multiply_subtract_fusion
  (274 shorter events, 102.7 us)
Async XLA Ops:
  7.2 286.5 %copy-start = (bf16[8,49,3072]{2,0,1:T(8,128)(2,1)S(1)}, bf16[8,49,3072]{2,0,1:T(8,128)(2,1)}, u32[]{:S(2)}) copy-start(bf16[8,49,3072]{2,0,1:T(8,128)(2,1)} %param.14) | copy-start | bytes 7225348
  7.2 7.0 copy-start.52
  7.2 203.1 %all-gather.2.cloned.1.call-start = ((), (), s32[]{:S(2)}) async-start(), calls=%async_computation.2 | async-start | bytes 34603008 | tf_op jit(solution)/shard_map/all_gather | solution.py:110
  10.2 507.7 %reduce-scatter.3.cloned.1.call-start = ((), (), s32[]{:S(2)}) async-start(), calls=%async_computation.3 | async-start | bytes 50331648 | tf_op jit(solution)/shard_map/reduce_scatter | solution.py:318
  13.6 284.2 %copy-start.26 = (f32[1,1024]{1,0:T(1,128)}, f32[1,1024]{1,0:T(1,128)S(1)}, u32[]{:S(2)}) copy-start(f32[1,1024]{1,0:T(1,128)S(1)} %get-tuple-element.68) | copy-start | bytes 12292
  13.6 304.9 %copy-start.36 = (f32[1,1024]{1,0:T(1,128)}, f32[1,1024]{1,0:T(1,128)S(1)}, u32[]{:S(2)}) copy-start(f32[1,1024]{1,0:T(1,128)S(1)} %get-tuple-element.62) | copy-start | bytes 12292
  13.6 315.9 %copy-start.34 = (f32[1,1024]{1,0:T(1,128)}, f32[1,1024]{1,0:T(1,128)S(1)}, u32[]{:S(2)}) copy-start(f32[1,1024]{1,0:T(1,128)S(1)} %get-tuple-element.71) | copy-start | bytes 12292
  13.6 319.0 %copy-start.28 = (f32[1,1024]{1,0:T(1,128)}, f32[1,1024]{1,0:T(1,128)S(1)}, u32[]{:S(2)}) copy-start(f32[1,1024]{1,0:T(1,128)S(1)} %get-tuple-element.60) | copy-start | bytes 12292
  280.3 18.0 %copy-start.4 = (bf16[64,16,1024]{2,1,0:T(8,128)(2,1)}, bf16[64,16,1024]{2,1,0:T(8,128)(2,1)S(1)}, u32[]{:S(2)}) copy-start(bf16[64,16,1024]{2,1,0:T(8,128)(2,1)S(1)} %get-tuple-element.56) | copy-start | bytes 6291460
  280.3 13.4 slice-start
  318.2 19.4 %copy-start.50 = (f32[8]{0:T(128)}, f32[8]{0:T(128)S(1)}, u32[]{:S(2)}) copy-start(f32[8]{0:T(128)S(1)} %broadcast_multiply_fusion.2) | copy-start | bytes 100
  318.4 19.2 %copy-start.57 = (f32[8]{0:T(128)}, f32[8]{0:T(128)S(1)}, u32[]{:S(2)}) copy-start(f32[8]{0:T(128)S(1)} %fusion.65) | copy-start | bytes 100
  318.5 11.0 copy-start.7
  318.5 14.4 %slice-start.3 = ((s8[8388608]{0:T(1024)(128)(4,1)}), s8[4194304]{0:T(1024)(128)(4,1)S(1)}, s32[]{:S(2)}) async-start(s8[8388608]{0:T(1024)(128)(4,1)} %bitcast.164), calls=%async_computation.9 | async-start | bytes 8388608
  324.4 8.5 slice-start.4
  324.4 11.4 slice-start.1
  369.8 9.8 copy-start.27
  428.5 22.9 %copy-start.64 = (pred[512]{0:T(512)(128)(4,1)S(1)}, pred[512]{0:T(512)(128)(4,1)}, u32[]{:S(2)}) copy-start(pred[512]{0:T(512)(128)(4,1)} %compare_and_fusion.1) | copy-start | bytes 1540
  474.4 747.2 %reduce-scatter.5.cloned.1.call-start = ((), (), s32[]{:S(2)}) async-start(), calls=%async_computation.4 | async-start | bytes 35651584 | tf_op jit(solution)/shard_map/reduce_scatter | solution.py:321
  536.8 821.8 %all-reduce.5.cloned.1.call-start = ((), (), s32[]{:S(2)}) async-start(), calls=%async_computation.5 | async-start | bytes 589824 | tf_op jit(solution)/shard_map/psum | solution.py:316
  540.3 862.8 %copy-start.13 = (f32[66,1024]{1,0:T(8,128)S(1)}, f32[66,1024]{1,0:T(8,128)}, u32[]{:S(2)}) copy-start(f32[66,1024]{1,0:T(8,128)} %param.22) | copy-start | bytes 811012
  540.3 862.8 %copy-start.17 = (f32[66,1024]{1,0:T(8,128)S(1)}, f32[66,1024]{1,0:T(8,128)}, u32[]{:S(2)}) copy-start(f32[66,1024]{1,0:T(8,128)} %param.24) | copy-start | bytes 811012
  540.3 862.8 %copy-start.18 = (f32[66,1024]{1,0:T(8,128)S(1)}, f32[66,1024]{1,0:T(8,128)}, u32[]{:S(2)}) copy-start(f32[66,1024]{1,0:T(8,128)} %param.23) | copy-start | bytes 811012
  1405.1 7.7 copy-start.1
  (53 other events, 194.3 us)
Sparse Core Ops, SparseCore 0:
  11.5 198.7 all-gather.1
  474.5 43.3 reduce-scatter.2
  536.9 684.6 reduce-scatter.4
  1227.3 131.2 all-reduce.4
where the time goes:
time: 1430 us; the launch traced here: 1420 us
  waiting for transfers between devices  1000 us (70%)
  local copies, waits for them, and re-layouts  133 us (9%)
  other arithmetic  103 us (7%)
  blocking collectives  89.8 us (6%)
  matrix products  74.5 us (5%)
  between operations  18.9 us (1%)
    reduce_scatter x1, waiting for transfers between devices, per_device(): owned = lax.psum_scatter(core_half, 'img', scatter_dimension=0, tiled=True)  676 us
    all_gather x1, waiting for transfers between devices, per_device(): lax.all_gather(cast_bfloat_narrow(masters), ('img', 'seq'), axis=0, tiled...  147 us
    psum x1, waiting for transfers between devices, per_device(): small_total, loss = lax.psum((small_grad, loss_part), ('img', 'seq'))  134 us
    all_gather x1, blocking collectives, per_device(): lax.all_gather(partner_emb, ('img', 'seq'), axis=0, tiled=True)  48.5 us
    reduce_scatter x1, waiting for transfers between devices, per_device(): lax.psum_scatter(slot_grads.astype(jnp.bfloat16), 'seq', scatter_dimensio...  43.5 us
    psum x1, blocking collectives, per_device(): owner_total = lax.psum(owner_squares, ('img', 'seq'))  41.4 us
    gather x1, local copies, waits for them, and re-layouts, per_device(): jnp.take(gathered, rows_index, axis=0)  35.4 us
  transfers between devices with their start and end apart: 4, of which 4 were waited for; matrix products, arithmetic and copies ran while one was open for 1% of the time, Pallas kernels for 0%

commit v1 on v0

--- a/solution.py
+++ b/solution.py
@@ -20,6 +20,35 @@
 DECAY_RATE = 0.05
 ADAM_EPS = 1e-08
 MASKED = -1000000000.0
+
+
+def view_table(a0, dim_no):
+    a0 = jnp.moveaxis(a0, 0, dim_no)
+    found_now = a0.shape
+    return a0.reshape(
+        *found_now[:dim_no], found_now[dim_no] * found_now[dim_no + 1], *found_now[dim_no + 2 :]
+    )
+
+
+def extend_spot_for(content, comm_axis):
+    world_n = lax.axis_size(comm_axis)
+    earlier = content[None]
+    for s in range(world_n.bit_length() - 1):
+        x_new = 1 << s
+        x_now = range(world_n)
+        heard = map(lambda dev_i: (dev_i, dev_i ^ x_new), x_now)
+        before = list(heard)
+        tmp = lax.ppermute(earlier, comm_axis, before)
+        piece_next = jnp.stack([earlier, tmp])
+        parts_out = lax.axis_index(comm_axis)
+        clean = parts_out >> s & 1
+        earlier = jnp.where(clean == 0, piece_next, piece_next[::-1]).reshape(-1, *content.shape)
+    return earlier
+
+
+def _turn_plate(block_in, work_x, join_dim):
+    mat_out = extend_spot_for(block_in, work_x)
+    return view_table(mat_out, join_dim)
 
 
 def layer_norm(values, gain, shift):
@@ -107,7 +136,7 @@
     slot_total = slot_unit_index.shape[0]
     img_dev = pixels.shape[0]
     scale = HEAD_DIM ** (-0.5)
-    gathered = lax.all_gather(cast_bfloat_narrow(masters), ("img", "seq"), axis=0, tiled=True)
+    gathered = _turn_plate(cast_bfloat_narrow(masters), ("img", "seq"), 0)
     unit_slot_index = (
         jnp.zeros((slot_total,), jnp.int32)
         .at[slot_unit_index]

time: 1430 us -> 2290 us (1.60)
  blocking collectives: 89.8 us -> 786 us
  other arithmetic: 103 us -> 216 us
  waiting for transfers between devices: 1000 us -> 1040 us
    all_gather x1, blocking collectives: 48.5 us -> 741 us  [per_device(): lax.all_gather(partner_emb, ('img', 'seq'), axis=0, tiled=True)]
    ppermute x0 -> x5, waiting for transfers between devices: none -> 319 us  [extend_spot_for(): tmp = lax.ppermute(earlier, comm_axis, before)]
    all_gather x1 -> x0, waiting for transfers between devices: 147 us -> none  [per_device(): lax.all_gather(cast_bfloat_narrow(masters), ('img', 'seq'), axis=0, tiled...]
    psum x1, waiting for transfers between devices: 134 us -> 0.01 us  [per_device(): small_total, loss = lax.psum((small_grad, loss_part), ('img', 'seq'))]
    select_n x0 -> x4, other arithmetic: none -> 61.6 us  [extend_spot_for(): jnp.where(clean == 0, piece_next, piece_next[::-1])]
    another operation x4 -> x11, other arithmetic: 2.25 us -> 49.5 us  [the longest x7 48.5 us: extend_spot_for(): piece_next = jnp.stack([earlier, tmp])]
  transfers between devices with their start and end apart: 4 -> 8, of which waited for: 4 -> 6; matrix products, arithmetic and copies ran while one was open for 1% -> 1% of each run, Pallas kernels for 0% -> 0%
where the time goes in v1:
time: 2290 us; the launch traced here: 2280 us
  waiting for transfers between devices  1040 us (45%)
  blocking collectives  786 us (34%)
  other arithmetic  216 us (9%)
  local copies, waits for them, and re-layouts  138 us (6%)
  matrix products  73.9 us (3%)
    all_gather x1, blocking collectives, per_device(): lax.all_gather(partner_emb, ('img', 'seq'), axis=0, tiled=True)  741 us
    reduce_scatter x1, waiting for transfers between devices, per_device(): owned = lax.psum_scatter(core_half, 'img', scatter_dimension=0, tiled=True)  672 us
    ppermute x5, waiting for transfers between devices, extend_spot_for(): tmp = lax.ppermute(earlier, comm_axis, before)  319 us
    select_n x4, other arithmetic, extend_spot_for(): jnp.where(clean == 0, piece_next, piece_next[::-1])  61.6 us
    another operation x7, other arithmetic, extend_spot_for(): piece_next = jnp.stack([earlier, tmp])  48.5 us
  transfers between devices with their start and end apart: 8, of which 6 were waited for; matrix products, arithmetic and copies ran while one was open for 1% of the time, Pallas kernels for 0%

profile of v1, /device:TPU:0, one launch (start us, length us, event | category | flops | bytes accessed | tf_op | source)
XLA Modules:
  0.0 2279.4 jit_solution(12853028170531860964)
XLA Ops:
  21.3 46.2 %collective-permute-done.1 = bf16[2,32,16,1024]{3,2,1,0:T(8,128)(2,1)} collective-permute-done((bf16[2,32,16,1024]{3,2,1,0:T(8,128)(2,1)}, bf16[2,32,16,1024]{3,2,1,0:T(8,128)(2,1)}, u32[]{:S(2)}, u32[]{:S(2)}) %collective-permute-start.1) | collective-permute-done | bytes 2097184 | tf_op jit(solution)/shard_map/ppermute | solution.py:41
  75.1 90.6 %collective-permute-done.2 = bf16[4,32,16,1024]{3,2,1,0:T(8,128)(2,1)} collective-permute-done((bf16[4,32,16,1024]{3,2,1,0:T(8,128)(2,1)}, bf16[4,32,16,1024]{3,2,1,0:T(8,128)(2,1)}, u32[]{:S(2)}, u32[]{:S(2)}) %collective-permute-start.2) | collective-permute-done | bytes 4194336 | tf_op jit(solution)/shard_map/ppermute | solution.py:41
  165.8 7.5 pad_maximum_fusion.2
  173.2 14.4 reverse_select_fusion.2
  189.1 179.9 %collective-permute-done.3 = bf16[8,32,16,1024]{3,2,1,0:T(8,128)(2,1)} collective-permute-done((bf16[8,32,16,1024]{3,2,1,0:T(8,128)(2,1)}, bf16[8,32,16,1024]{3,2,1,0:T(8,128)(2,1)}, u32[]{:S(2)}, u32[]{:S(2)}) %collective-permute-start.3) | collective-permute-done | bytes 8388640 | tf_op jit(solution)/shard_map/ppermute | solution.py:41
  369.0 8.0 pad_maximum_fusion.1
  377.1 10.6 reverse_select_fusion.1
  395.0 741.4 %all_gather.3 = bf16[256,768]{1,0:T(8,128)(2,1)} all-gather(bf16[8,768]{1,0:T(8,128)(2,1)S(1)} %copy-done.55), channel_id=1, replica_groups=mesh['img'=16,'seq'=2] {'img','seq'}, dimensions={0}, use_global_device_ids=true | all-gather | bytes 405504 | tf_op jit(solution)/shard_map/all_gather | solution.py:212
  1137.0 23.2 %pad_maximum_fusion = bf16[2,16,32,16,1024]{4,3,2,1,0:T(8,128)(2,1)} fusion(bf16[1,16,32,16,1024]{4,3,2,1,0:T(8,128)(2,1)} %bitcast.15, bf16[1,16,32,16,1024]{4,3,2,1,0:T(8,128)(2,1)} %bitcast.13), kind=kLoop, calls=%fused_computation.6 | loop fusion | flops 16777216 | bytes 67108864 | tf_op jit(solution)/shard_map/stack | solution.py:42
  1160.2 33.4 %reverse_select_fusion = bf16[2,16,32,16,1024]{4,3,2,1,0:T(8,128)(2,1)} fusion(bf16[2,16,32,16,1024]{4,3,2,1,0:T(8,128)(2,1)} %pad_maximum_fusion, pred[]{:T(512)S(6)} %eq.30), kind=kLoop, calls=%fused_computation.5 | loop fusion | flops 16777216 | bytes 67108864 | tf_op jit(solution)/shard_map/jit(_where)/select_n | solution.py:45
  1193.6 35.4 %gather_fusion = bf16[1008,16,1024]{2,1,0:T(8,128)(2,1)} fusion(bf16[1024,16,1024]{2,1,0:T(8,128)(2,1)} %bitcast.177, s32[1024]{0:T(1024)S(1)} %get-tuple-element.99), kind=kCustom, calls=%fused_computation | custom fusion | bytes 66064320 | tf_op jit(solution)/shard_map/jit(_take)/gather | solution.py:149
  1229.0 22.6 broadcast_select_fusion
  1254.2 6.6 fusion.83
  1260.8 12.6 fusion.82
  1371.7 6.9 convolution_bitcast_fusion
  1378.6 8.7 copy.40
  1413.9 22.9 %gather_fusion.1 = bf16[512,32,1024]{2,1,0:T(8,128)(2,1)} fusion(bf16[504,32,1024]{2,1,0:T(8,128)(2,1)} %bitcast.187, s32[1024]{0:T(1024)S(1)} %copy-done.56), kind=kCustom, calls=%fused_computation.1 | custom fusion | bytes 67110912 | tf_op jit(solution)/shard_map/jit(_take)/gather | solution.py:346
  1436.8 23.0 %select_convert_fusion = bf16[512,32,1024]{2,1,0:T(8,128)(2,1)} fusion(bf16[512,32,1024]{2,1,0:T(8,128)(2,1)} %gather_fusion.1, pred[512]{0:T(512)(128)(4,1)S(1)} %copy-done.66), kind=kLoop, calls=%fused_computation.4 | loop fusion | flops 16777216 | bytes 67109376 | tf_op jit(solution)/shard_map/convert_element_type | solution.py:348
  1459.9 45.1 %reduce-scatter.3.cloned.1.call-done = bf16[512,16,1024]{2,1,0:T(8,128)(2,1)} async-done(((bf16[512,32,1024]{2,1,0:T(8,128)(2,1)}), bf16[512,16,1024]{2,1,0:T(8,128)(2,1)}) %reduce-scatter.3.cloned.1.call-update) | async-done | bytes 16777232 | tf_op jit(solution)/shard_map/reduce_scatter | solution.py:347
  1505.0 18.7 convert_element_type.124
  1530.8 6.2 concatenate.17
  1539.0 671.9 %reduce-scatter.5.cloned.1.call-done = f32[32,16,1024]{2,1,0:T(8,128)} async-done(((f32[512,16,1024]{2,1,0:T(8,128)}), f32[32,16,1024]{2,1,0:T(8,128)}) %reduce-scatter.5.cloned.1.call-update) | async-done | bytes 2097168 | tf_op jit(solution)/shard_map/reduce_scatter | solution.py:350
  2215.2 44.2 %all-reduce.2 = (f32[]{:T(128)}, f32[]{:T(128)}) all-reduce(f32[]{:T(128)} %multiply_reduce_fusion, f32[]{:T(128)S(6)} %div.166), channel_id=1, replica_groups=mesh['img'=16,'seq'=2] {'img','seq'}, use_global_device_ids=true, to_apply=%region_23.24 | all-reduce | flops 2 | bytes 16 | tf_op jit(solution)/shard_map/psum | solution.py:352
  2262.9 7.6 multiply_subtract_fusion
  (292 shorter events, 171.3 us)
Async XLA Ops:
  8.0 1268.2 %copy-start = (bf16[8,49,3072]{2,0,1:T(8,128)(2,1)S(1)}, bf16[8,49,3072]{2,0,1:T(8,128)(2,1)}, u32[]{:S(2)}) copy-start(bf16[8,49,3072]{2,0,1:T(8,128)(2,1)} %param.14) | copy-start | bytes 7225348
  8.0 1497.0 %reduce-scatter.3.cloned.1.call-start = ((), (), s32[]{:S(2)}) async-start(), calls=%async_computation.2 | async-start | bytes 50331648 | tf_op jit(solution)/shard_map/reduce_scatter | solution.py:347
  11.0 3.1 collective-permute-start
  18.4 49.1 %collective-permute-start.1 = (bf16[2,32,16,1024]{3,2,1,0:T(8,128)(2,1)}, bf16[2,32,16,1024]{3,2,1,0:T(8,128)(2,1)}, u32[]{:S(2)}, u32[]{:S(2)}) collective-permute-start(bf16[2,32,16,1024]{3,2,1,0:T(8,128)(2,1)} %get-tuple-element.59), channel_id=1, source_target_pairs={{0,2},{1,3},{2,0},{3,1},{4,6},{5,7},{6,4},{7,5},{8,10},{9,11},{10,... | collective-permute-start | bytes 6291464 | tf_op jit(solution)/shard_map/ppermute | solution.py:41
  73.4 92.4 %collective-permute-start.2 = (bf16[4,32,16,1024]{3,2,1,0:T(8,128)(2,1)}, bf16[4,32,16,1024]{3,2,1,0:T(8,128)(2,1)}, u32[]{:S(2)}, u32[]{:S(2)}) collective-permute-start(bf16[4,32,16,1024]{3,2,1,0:T(8,128)(2,1)} %bitcast.8), channel_id=1, source_target_pairs={{0,4},{1,5},{2,6},{3,7},{4,0},{5,1},{6,2},{7,3},{8,12},{9,13},{10,... | collective-permute-start | bytes 12582920 | tf_op jit(solution)/shard_map/ppermute | solution.py:41
  187.6 181.4 %collective-permute-start.3 = (bf16[8,32,16,1024]{3,2,1,0:T(8,128)(2,1)}, bf16[8,32,16,1024]{3,2,1,0:T(8,128)(2,1)}, u32[]{:S(2)}, u32[]{:S(2)}) collective-permute-start(bf16[8,32,16,1024]{3,2,1,0:T(8,128)(2,1)} %bitcast.188), channel_id=1, source_target_pairs={{0,8},{1,9},{2,10},{3,11},{4,12},{5,13},{6,14},{7,15},{8,0},{9,1},... | collective-permute-start | bytes 25165832 | tf_op jit(solution)/shard_map/ppermute | solution.py:41
  377.0 12.9 copy-start.59
  377.0 15.9 copy-start.12
  377.0 15.9 copy-start.65
  377.0 18.0 copy-start.55
  387.7 749.3 %collective-permute-start.4 = (bf16[16,32,16,1024]{3,2,1,0:T(8,128)(2,1)}, bf16[16,32,16,1024]{3,2,1,0:T(8,128)(2,1)}, u32[]{:S(2)}, u32[]{:S(2)}) collective-permute-start(bf16[16,32,16,1024]{3,2,1,0:T(8,128)(2,1)} %bitcast.14), channel_id=1, source_target_pairs={{0,16},{1,17},{2,18},{3,19},{4,20},{5,21},{6,22},{7,23},{8,24},{9,... | collective-permute-start | bytes 50331656 | tf_op jit(solution)/shard_map/ppermute | solution.py:41
  394.4 885.1 %copy-start.42 = (f32[1,1024]{1,0:T(1,128)}, f32[1,1024]{1,0:T(1,128)S(1)}, u32[]{:S(2)}) copy-start(f32[1,1024]{1,0:T(1,128)S(1)} %get-tuple-element.74) | copy-start | bytes 12292
  394.4 885.9 %copy-start.26 = (f32[1,1024]{1,0:T(1,128)}, f32[1,1024]{1,0:T(1,128)S(1)}, u32[]{:S(2)}) copy-start(f32[1,1024]{1,0:T(1,128)S(1)} %get-tuple-element.72) | copy-start | bytes 12292
  1254.2 26.7 %copy-start.7 = (bf16[128,16,1024]{2,1,0:T(8,128)(2,1)}, bf16[128,16,1024]{2,1,0:T(8,128)(2,1)S(1)}, u32[]{:S(2)}) copy-start(bf16[128,16,1024]{2,1,0:T(8,128)(2,1)S(1)} %slice.177) | copy-start | bytes 12582916
  1260.8 15.4 slice-start
  1304.3 19.5 copy-start.53
  1304.5 19.2 copy-start.60
  1304.6 14.4 slice-start.3
  1413.9 22.9 %copy-start.66 = (pred[512]{0:T(512)(128)(4,1)S(1)}, pred[512]{0:T(512)(128)(4,1)}, u32[]{:S(2)}) copy-start(pred[512]{0:T(512)(128)(4,1)} %compare_and_fusion.1) | copy-start | bytes 1540
  1459.8 751.0 %reduce-scatter.5.cloned.1.call-start = ((), (), s32[]{:S(2)}) async-start(), calls=%async_computation.3 | async-start | bytes 35651584 | tf_op jit(solution)/shard_map/reduce_scatter | solution.py:350
  1523.7 689.9 %all-reduce.5.cloned.1.call-start = ((), (), s32[]{:S(2)}) async-start(), calls=%async_computation.4 | async-start | bytes 589824 | tf_op jit(solution)/shard_map/psum | solution.py:345
  1530.7 730.1 %copy-start.13 = (f32[66,1024]{1,0:T(8,128)S(1)}, f32[66,1024]{1,0:T(8,128)}, u32[]{:S(2)}) copy-start(f32[66,1024]{1,0:T(8,128)} %param.22) | copy-start | bytes 811012
  1530.7 730.1 %copy-start.16 = (f32[66,1024]{1,0:T(8,128)S(1)}, f32[66,1024]{1,0:T(8,128)}, u32[]{:S(2)}) copy-start(f32[66,1024]{1,0:T(8,128)} %param.24) | copy-start | bytes 811012
  1530.7 730.1 %copy-start.17 = (f32[66,1024]{1,0:T(8,128)S(1)}, f32[66,1024]{1,0:T(8,128)}, u32[]{:S(2)}) copy-start(f32[66,1024]{1,0:T(8,128)} %param.23) | copy-start | bytes 811012
  (58 other events, 250.2 us)
Sparse Core Ops, SparseCore 0:
  1459.9 44.9 reduce-scatter.2
  1523.8 687.0 reduce-scatter.4
Sparse Core Ops, SparseCore 1:
  1537.1 302.0 all-reduce.4
